TPU v7x, 32 devices: a whole 2x2x4 slice. The times are simulated.
32 devices in a mesh: groups: 2 (over x), tile: 8 (over z, y), freq: 2 (over core).
Axes of the slice: x: 2, y: 2, z: 4, core: 2. Of those that a mesh axis runs over, the one named last changes fastest.
Arguments:
- panels: bfloat16 [8, 2, 256, 384], P('freq'), may hold values from -0.3125 to 0.3125
- snapshots: bfloat16 [16, 2, 32, 256], P(('groups', 'freq')), parts along dimension 0, may hold values from -6 to 6
- wavenumbers: float32 [8, 384], P('freq'), may hold values from 0.05 to 0.5
- mode_counts: int32 [8], P('freq'), may hold values from 48 to 384, as said below
- mode_mask: int32 [8, 3, 64], P('freq'), may hold values from 0 to 1, as said below
- mode_shapes: bfloat16 [8, 2048, 384], P('freq', 'tile'), may hold values from -6 to 6
Outputs:
- surface: float32 [32, 2048], P(('groups', 'tile', 'freq')), parts along dimension 0
There are 2 independent parts, one for each index of `groups`. A program takes and returns all parts, laid end to end along the dimension named above; an argument that names none is the same for every part. Nothing has to cross between parts.
Inputs may be any that keep to these rules, and one draw needn't show every extreme that they name: `mode_counts`: some frequency has exactly 384 modes and some exactly 48. `mode_mask`: mode block 0 is live in every depth block of every frequency.
All inputs are finite; a program needn't handle non-finite values.
Results may differ from a plain program's by a relative error of at most 0.0005.
Values may be sent and summed in bfloat16 or wider, within the bound.
A program may use at most 64 MiB of HBM per device.

v0:
```python
import functools

import jax
import jax.numpy as jnp
from jax import lax
from jax.experimental import pallas as pl
from jax.experimental.pallas import tpu as pltpu
from jax.sharding import PartitionSpec as P

MBLK = 128
ZBLK = 32
MESH = pl.DeviceIdType.MESH

range_anchor = 1000.0
range_step = 25.0


def cosine_and_sine(angle):
    turns = jnp.floor(angle * 0.6366197723675814 + 0.5)
    rest = ((angle - turns * 1.5703125) - turns * 4.837512969970703125e-4) - (
        turns * 7.54978995489188216e-8
    )
    quarter = turns.astype(jnp.int32)
    square = rest * rest
    sine = rest + rest * square * (
        -1.6666654611e-1 + square * (8.3321608736e-3 - square * 1.9515295891e-4)
    )
    cosine = (1.0 - 0.5 * square) + square * square * (
        4.166664568298827e-2
        + square * (-1.388731625493765e-3 + square * 2.443315711809948e-5)
    )
    odd = (quarter & 1) == 1
    first = jnp.where(odd, sine, cosine)
    second = jnp.where(odd, cosine, sine)
    first = jnp.where(((quarter + 1) & 2) == 2, -first, first)
    second = jnp.where((quarter & 2) == 2, -second, second)
    return first, second


def surface_kernel(
    sizes,
    all_freqs,
    counts,
    mask_hbm,
    panels_hbm,
    snaps_hbm,
    wavenumbers_hbm,
    shapes_hbm,
    out,
    mask,
    panels,
    snaps,
    wavenumbers,
    shapes,
    cosines,
    sines,
    lhs_a,
    lhs_b,
    weights,
    energy,
    probe,
    panel_probe,
    power,
    rows_out,
    rows_in,
    table_sem,
    panel_sem,
    snap_sem,
    shape_sem,
    energy_send,
    energy_recv,
    row_send,
    row_recv,
):
    groups, tiles, freqs = sizes
    freq_count, depth_count, modes = shapes.shape
    receivers = panels.shape[2]
    snap_count = snaps.shape[2]
    ranges = cosines.shape[1]
    own_ranges = ranges // groups
    chunk = receivers // own_ranges
    group = lax.axis_index("groups")
    tile = lax.axis_index("tile")
    freq = lax.axis_index("freq")
    peers = tiles * freqs
    me = tile * freqs + freq

    number_copy = pltpu.make_async_copy(wavenumbers_hbm, wavenumbers, table_sem.at[0])
    number_copy.start()
    panel_copies, snap_copies, shape_copies = [], [], []
    for f in range(freq_count):
        panel_copies.append(
            pltpu.make_async_copy(panels_hbm.at[f], panels.at[f], panel_sem.at[f])
        )
        shape_copies.append(
            pltpu.make_async_copy(shapes_hbm.at[f], shapes.at[f], shape_sem.at[f])
        )
        snap_copies.append(pltpu.make_async_copy(snaps_hbm.at[f], snaps.at[f], snap_sem.at[f]))
    mask_copy = pltpu.make_async_copy(mask_hbm, mask, table_sem.at[1])
    panel_copies[0].start()
    mask_copy.start()
    for f in range(freq_count):
        shape_copies[f].start()
        snap_copies[f].start()
        if f + 1 < freq_count:
            panel_copies[f + 1].start()

    barrier = pltpu.get_barrier_semaphore()
    for step in range(1, peers):
        other = lax.rem(me + step, peers)
        pl.semaphore_signal(
            barrier,
            inc=1,
            device_id=(group, lax.div(other, freqs), lax.rem(other, freqs)),
            device_id_type=MESH,
        )
    for step in range(1, groups):
        pl.semaphore_signal(
            barrier,
            inc=1,
            device_id=(lax.rem(group + step, groups), tile, freq),
            device_id_type=MESH,
        )

    number_copy.wait()
    index = lax.broadcasted_iota(jnp.int32, (ranges, modes), 0)
    distance = range_anchor + range_step * index.astype(jnp.float32)
    for f in range(freq_count):
        c, s = cosine_and_sine(distance * wavenumbers[pl.ds(f, 1), :])
        cosines[f] = c
        sines[f] = s
    mask_copy.wait()

    block_count = mask.shape[2]
    depth_block = (
        lax.broadcasted_iota(jnp.int32, (block_count, depth_count), 1) + tile * depth_count
    ) // ZBLK
    one_hot = (
        depth_block == lax.broadcasted_iota(jnp.int32, (block_count, depth_count), 0)
    ).astype(jnp.bfloat16)
    mode_index = lax.broadcasted_iota(jnp.int32, (MBLK, depth_count), 0)

    def live_shapes(f):
        flags = mask[:, f, :].astype(jnp.float32).astype(jnp.bfloat16)
        live = jnp.dot(flags, one_hot, preferred_element_type=jnp.float32)
        for block in range(modes // MBLK):
            columns = pl.ds(block * MBLK, MBLK)
            inside = (mode_index + block * MBLK) < counts[f]
            keep = jnp.where(inside, live[block : block + 1, :], 0.0).astype(jnp.bfloat16)
            weights[f, columns, :] = shapes[f, :, columns].T * keep

    first = group * own_ranges
    buffers = (lhs_a, lhs_b)
    piece = 16

    def turn(f, buffer, j):
        for start in range(0, chunk, piece):
            base = j * chunk + start
            rows = pl.ds(pl.multiple_of(base, piece), piece)
            imag_rows = pl.ds(pl.multiple_of(receivers + base, piece), piece)
            real = panels[f, 0, rows, :].astype(jnp.float32)
            imag = panels[f, 1, rows, :].astype(jnp.float32)
            for r in range(own_ranges):
                c = cosines[f, pl.ds(first + r, 1), :]
                s = sines[f, pl.ds(first + r, 1), :]
                buffer[r, rows, :] = (real * c - imag * s).astype(jnp.bfloat16)
                buffer[r, imag_rows, :] = (imag * c + real * s).astype(jnp.bfloat16)

    def measure_energy(f, buffer, j):
        replica = jnp.dot(buffer[j], weights[f], preferred_element_type=jnp.float32)
        total = jnp.sum(replica * replica, axis=0, keepdims=True)
        energy[group, f, pl.ds(j, 1), :] = total / receivers + 1e-6

    def project_panels(f):
        pair = snaps[f].reshape(2 * snap_count, receivers)
        on_real = jnp.dot(pair, panels[f, 0], preferred_element_type=jnp.float32)
        on_imag = jnp.dot(pair, panels[f, 1], preferred_element_type=jnp.float32)
        panel_probe[0] = on_real[:snap_count] + on_imag[snap_count:]
        panel_probe[1] = on_imag[:snap_count] - on_real[snap_count:]

    def turn_probe(f, j):
        real, imag = panel_probe[0], panel_probe[1]
        for i in range(groups):
            r = j * groups + i
            c = cosines[f, pl.ds(r, 1), :]
            s = sines[f, pl.ds(r, 1), :]
            probe[f, r, pl.ds(0, snap_count), :] = (real * c - imag * s).astype(jnp.bfloat16)
            probe[f, r, pl.ds(snap_count, snap_count), :] = (imag * c + real * s).astype(
                jnp.bfloat16
            )

    for stage in range(freq_count + 1):
        if stage < freq_count:
            panel_copies[stage].wait()
        if stage > 0:
            shape_copies[stage - 1].wait()
            live_shapes(stage - 1)
            snap_copies[stage - 1].wait()
            project_panels(stage - 1)

        def body(j, carry, stage=stage):
            if stage < freq_count:
                turn(stage, buffers[stage % 2], j)
            if stage > 0:
                measure_energy(stage - 1, buffers[(stage - 1) % 2], j)
                turn_probe(stage - 1, j)
            return carry

        lax.fori_loop(0, own_ranges, body, 0)

    pl.semaphore_wait(barrier, peers - 1 + groups - 1)
    energy_copies = []
    for step in range(1, groups):
        energy_copies.append(
            pltpu.make_async_remote_copy(
                src_ref=energy.at[group],
                dst_ref=energy.at[group],
                send_sem=energy_send.at[step],
                recv_sem=energy_recv.at[step],
                device_id=(lax.rem(group + step, groups), tile, freq),
                device_id_type=MESH,
            )
        )
    for copy in energy_copies:
        copy.start()

    for f in range(freq_count):
        for start in range(0, ranges, own_ranges):
            left = probe[f, pl.ds(start, own_ranges)].reshape(-1, modes)
            projected = jnp.dot(left, weights[f], preferred_element_type=jnp.float32)
            squares = (projected * projected).reshape(own_ranges, 2 * snap_count, depth_count)
            power[f, pl.ds(start, own_ranges), :] = jnp.sum(squares, axis=1) / snap_count

    for copy in energy_copies:
        copy.wait()
    for g in range(groups):
        part = jnp.zeros((own_ranges, depth_count), jnp.float32)
        for f in range(freq_count):
            part += power[f, pl.ds(g * own_ranges, own_ranges), :] / (
                2.0 * receivers * energy[g, f]
            )
        for r in range(own_ranges):
            rows_out[g * own_ranges + r] = part[r : r + 1, :]

    row_copies = []
    for step in range(1, peers):
        other = lax.rem(me + step, peers)
        row_copies.append(
            pltpu.make_async_remote_copy(
                src_ref=rows_out.at[other],
                dst_ref=rows_in.at[me],
                send_sem=row_send.at[step],
                recv_sem=row_recv.at[step],
                device_id=(group, lax.div(other, freqs), lax.rem(other, freqs)),
                device_id_type=MESH,
            )
        )
    for copy in row_copies:
        copy.start()
    rows_in[me] = rows_out[me]
    for copy in row_copies:
        copy.wait()
    for t in range(tiles):
        total = rows_in[t * freqs]
        for f in range(1, freqs):
            total += rows_in[t * freqs + f]
        out[pl.ds(t, 1), :] = total / all_freqs


def on_device(panels, snapshots, wavenumbers, mode_counts, mode_mask, mode_shapes):
    groups, tiles, freqs = (lax.axis_size(name) for name in ("groups", "tile", "freq"))
    freq_count, depth_count, modes = mode_shapes.shape
    receivers = panels.shape[2]
    ranges = tiles * freqs
    own_ranges = ranges // groups
    snap_count = snapshots.shape[2]
    vmem = pl.BlockSpec(memory_space=pltpu.VMEM)
    smem = pl.BlockSpec(memory_space=pltpu.SMEM)
    hbm = pl.BlockSpec(memory_space=pltpu.HBM)
    by_block = jnp.swapaxes(mode_mask, 0, 1)
    inputs = (by_block, panels, snapshots, wavenumbers, mode_shapes)
    surface = pl.pallas_call(
        functools.partial(surface_kernel, (groups, tiles, freqs), freq_count * freqs),
        out_shape=jax.ShapeDtypeStruct((tiles, depth_count), jnp.float32),
        in_specs=[smem] + [hbm] * 5,
        out_specs=vmem,
        scratch_shapes=[pltpu.VMEM(value.shape, value.dtype) for value in inputs]
        + [
            pltpu.VMEM((freq_count, ranges, modes), jnp.float32),
            pltpu.VMEM((freq_count, ranges, modes), jnp.float32),
            pltpu.VMEM((own_ranges, 2 * receivers, modes), jnp.bfloat16),
            pltpu.VMEM((own_ranges, 2 * receivers, modes), jnp.bfloat16),
            pltpu.VMEM((freq_count, modes, depth_count), jnp.bfloat16),
            pltpu.VMEM((groups, freq_count, own_ranges, depth_count), jnp.float32),
            pltpu.VMEM((freq_count, ranges, 2 * snap_count, modes), jnp.bfloat16),
            pltpu.VMEM((2, snap_count, modes), jnp.float32),
            pltpu.VMEM((freq_count, ranges, depth_count), jnp.float32),
            pltpu.VMEM((ranges, 1, depth_count), jnp.float32),
            pltpu.VMEM((ranges, 1, depth_count), jnp.float32),
            pltpu.SemaphoreType.DMA((2,)),
            pltpu.SemaphoreType.DMA((freq_count,)),
            pltpu.SemaphoreType.DMA((freq_count,)),
            pltpu.SemaphoreType.DMA((freq_count,)),
            pltpu.SemaphoreType.DMA((groups,)),
            pltpu.SemaphoreType.DMA((groups,)),
            pltpu.SemaphoreType.DMA((ranges,)),
            pltpu.SemaphoreType.DMA((ranges,)),
        ],
        compiler_params=pltpu.CompilerParams(
            collective_id=0, has_side_effects=True, vmem_limit_bytes=56 * 1024 * 1024
        ),
    )(mode_counts, *inputs)
    return surface.reshape(1, tiles * depth_count)


def solution(mesh):
    in_specs = (
        P("freq", None, None, None),
        P(("groups", "freq"), None, None, None),
        P("freq", None),
        P("freq"),
        P("freq", None, None),
        P("freq", "tile", None),
    )
    out_specs = P(("groups", "tile", "freq"), None)
    return jax.shard_map(
        on_device, mesh=mesh, in_specs=in_specs, out_specs=out_specs, check_vma=False
    )
```

profile of v0, /device:TPU:0, one launch (start us, length us, event | category | flops | bytes accessed | tf_op | source)
XLA Modules:
  0.0 28.1 jit_solution(7531280503696901802)
XLA Ops:
  0.0 26.8 %shard_map.64 = f32[8,256]{1,0:T(8,128)} custom-call(s32[4]{0:T(128)} %counts.1, s32[3,4,64]{2,1,0:T(4,128)} %bitcast.5, bf16[4,2,256,384]{3,2,1,0:T(8,128)(2,1)} %panels_hbm.1, bf16[4,2,32,256]{3,2,1,0:T(8,128)(2,1)} %snaps_hbm.1, f32[4,384]{1,0:T(4,128)} %wavenumbers_hbm.1, bf16[4,256,384]{2,1,0:T(8,128)(2,1)} %shapes_hbm.1), custom_call_target="tpu_custom_call" | custom-call | tf_op jit(solution)/shard_map/pallas_call | solution.py:282
  26.8 1.3 %copy.7 = f32[1,1,8,256]{3,1,2,0:T(1,128)} copy(f32[1,1,8,256]{3,2,1,0:T(8,128)} %bitcast.4) | data formatting | bytes 16384
where the time goes:
time: 28.3 us; the launch traced here: 28.1 us
  Pallas kernels  26.8 us (95%)
  local copies, waits for them, and re-layouts  1.3 us (5%)
    pallas_call x1, Pallas kernels, on_device(): pl.pallas_call(functools.partial(surface_kernel, (groups, tiles, freqs),...  26.8 us
    unnamed x1, local copies, waits for them, and re-layouts  1.3 us

commit v1 on v0

--- a/solution.py
+++ b/solution.py
@@ -78,7 +78,10 @@
     snap_count = snaps.shape[2]
     ranges = cosines.shape[1]
     own_ranges = ranges // groups
-    chunk = receivers // own_ranges
+    per = min(2, own_ranges)
+    turns = own_ranges // per
+    chunk = receivers // turns
+    products = -(-2 * freq_count // turns)
     group = lax.axis_index("groups")
     tile = lax.axis_index("tile")
     freq = lax.axis_index("freq")
@@ -127,8 +130,9 @@
     distance = range_anchor + range_step * index.astype(jnp.float32)
     for f in range(freq_count):
         c, s = cosine_and_sine(distance * wavenumbers[pl.ds(f, 1), :])
-        cosines[f] = c
-        sines[f] = s
+        for r in range(ranges):
+            cosines[f, r] = jnp.broadcast_to(c[r : r + 1, :], (8, modes))
+            sines[f, r] = jnp.broadcast_to(s[r : r + 1, :], (8, modes))
     mask_copy.wait()
 
     block_count = mask.shape[2]
@@ -153,60 +157,78 @@
     buffers = (lhs_a, lhs_b)
     piece = 16
 
+    def rotate(real, imag, f, r):
+        c, s = cosines[f, r], sines[f, r]
+        return (
+            (real * c - imag * s).reshape(-1, modes).astype(jnp.bfloat16),
+            (imag * c + real * s).reshape(-1, modes).astype(jnp.bfloat16),
+        )
+
     def turn(f, buffer, j):
         for start in range(0, chunk, piece):
             base = j * chunk + start
             rows = pl.ds(pl.multiple_of(base, piece), piece)
             imag_rows = pl.ds(pl.multiple_of(receivers + base, piece), piece)
-            real = panels[f, 0, rows, :].astype(jnp.float32)
-            imag = panels[f, 1, rows, :].astype(jnp.float32)
+            real = panels[f, 0, rows, :].astype(jnp.float32).reshape(-1, 8, modes)
+            imag = panels[f, 1, rows, :].astype(jnp.float32).reshape(-1, 8, modes)
             for r in range(own_ranges):
-                c = cosines[f, pl.ds(first + r, 1), :]
-                s = sines[f, pl.ds(first + r, 1), :]
-                buffer[r, rows, :] = (real * c - imag * s).astype(jnp.bfloat16)
-                buffer[r, imag_rows, :] = (imag * c + real * s).astype(jnp.bfloat16)
+                buffer[r, rows, :], buffer[r, imag_rows, :] = rotate(real, imag, f, first + r)
 
     def measure_energy(f, buffer, j):
-        replica = jnp.dot(buffer[j], weights[f], preferred_element_type=jnp.float32)
-        total = jnp.sum(replica * replica, axis=0, keepdims=True)
-        energy[group, f, pl.ds(j, 1), :] = total / receivers + 1e-6
-
-    def project_panels(f):
-        pair = snaps[f].reshape(2 * snap_count, receivers)
-        on_real = jnp.dot(pair, panels[f, 0], preferred_element_type=jnp.float32)
-        on_imag = jnp.dot(pair, panels[f, 1], preferred_element_type=jnp.float32)
-        panel_probe[0] = on_real[:snap_count] + on_imag[snap_count:]
-        panel_probe[1] = on_imag[:snap_count] - on_real[snap_count:]
+        left = buffer[pl.ds(j * per, per)].reshape(per * 2 * receivers, modes)
+        replica = jnp.dot(left, weights[f], preferred_element_type=jnp.float32)
+        squares = (replica * replica).reshape(per, 2 * receivers, depth_count)
+        for i in range(per):
+            total = jnp.sum(squares[i], axis=0, keepdims=True)
+            energy[group, f, pl.ds(j * per + i, 1), :] = total / receivers + 1e-6
+
+    def project_panels(j):
+        for i in range(products):
+            step = j * products + i
+            f, half = lax.div(step, 2), lax.rem(step, 2)
+            pair = snaps[f].reshape(2 * snap_count, receivers)
+            panel_probe[f, half] = jnp.dot(
+                pair, panels[f, half], preferred_element_type=jnp.float32
+            )
 
     def turn_probe(f, j):
-        real, imag = panel_probe[0], panel_probe[1]
-        for i in range(groups):
-            r = j * groups + i
-            c = cosines[f, pl.ds(r, 1), :]
-            s = sines[f, pl.ds(r, 1), :]
-            probe[f, r, pl.ds(0, snap_count), :] = (real * c - imag * s).astype(jnp.bfloat16)
-            probe[f, r, pl.ds(snap_count, snap_count), :] = (imag * c + real * s).astype(
-                jnp.bfloat16
-            )
+        on_real, on_imag = panel_probe[f, 0], panel_probe[f, 1]
+        real = (on_real[:snap_count] + on_imag[snap_count:]).reshape(-1, 8, modes)
+        imag = (on_imag[:snap_count] - on_real[snap_count:]).reshape(-1, 8, modes)
+        for i in range(per * groups):
+            r = j * per * groups + i
+            top, bottom = rotate(real, imag, f, r)
+            probe[f, r, pl.ds(0, snap_count), :] = top
+            probe[f, r, pl.ds(snap_count, snap_count), :] = bottom
 
     for stage in range(freq_count + 1):
-        if stage < freq_count:
+        if stage < min(2, freq_count):
             panel_copies[stage].wait()
         if stage > 0:
             shape_copies[stage - 1].wait()
             live_shapes(stage - 1)
-            snap_copies[stage - 1].wait()
-            project_panels(stage - 1)
-
-        def body(j, carry, stage=stage):
+        if stage == 1:
+            for copy in panel_copies[2:] + snap_copies:
+                copy.wait()
+        if stage < 2:
+            probes = []
+        elif stage < freq_count:
+            probes = [stage - 2]
+        else:
+            probes = list(range(freq_count - 2, freq_count))
+
+        def body(j, carry, stage=stage, probes=probes):
+            if stage > 0:
+                measure_energy(stage - 1, buffers[(stage - 1) % 2], j)
             if stage < freq_count:
                 turn(stage, buffers[stage % 2], j)
-            if stage > 0:
-                measure_energy(stage - 1, buffers[(stage - 1) % 2], j)
-                turn_probe(stage - 1, j)
+            if stage == 1:
+                project_panels(j)
+            for f in probes:
+                turn_probe(f, j)
             return carry
 
-        lax.fori_loop(0, own_ranges, body, 0)
+        lax.fori_loop(0, turns, body, 0)
 
     pl.semaphore_wait(barrier, peers - 1 + groups - 1)
     energy_copies = []
@@ -264,7 +286,7 @@
         total = rows_in[t * freqs]
         for f in range(1, freqs):
             total += rows_in[t * freqs + f]
-        out[pl.ds(t, 1), :] = total / all_freqs
+        out[t] = total / all_freqs
 
 
 def on_device(panels, snapshots, wavenumbers, mode_counts, mode_mask, mode_shapes):
@@ -281,19 +303,19 @@
     inputs = (by_block, panels, snapshots, wavenumbers, mode_shapes)
     surface = pl.pallas_call(
         functools.partial(surface_kernel, (groups, tiles, freqs), freq_count * freqs),
-        out_shape=jax.ShapeDtypeStruct((tiles, depth_count), jnp.float32),
+        out_shape=jax.ShapeDtypeStruct((tiles, 1, depth_count), jnp.float32),
         in_specs=[smem] + [hbm] * 5,
         out_specs=vmem,
         scratch_shapes=[pltpu.VMEM(value.shape, value.dtype) for value in inputs]
         + [
-            pltpu.VMEM((freq_count, ranges, modes), jnp.float32),
-            pltpu.VMEM((freq_count, ranges, modes), jnp.float32),
+            pltpu.VMEM((freq_count, ranges, 8, modes), jnp.float32),
+            pltpu.VMEM((freq_count, ranges, 8, modes), jnp.float32),
             pltpu.VMEM((own_ranges, 2 * receivers, modes), jnp.bfloat16),
             pltpu.VMEM((own_ranges, 2 * receivers, modes), jnp.bfloat16),
             pltpu.VMEM((freq_count, modes, depth_count), jnp.bfloat16),
             pltpu.VMEM((groups, freq_count, own_ranges, depth_count), jnp.float32),
             pltpu.VMEM((freq_count, ranges, 2 * snap_count, modes), jnp.bfloat16),
-            pltpu.VMEM((2, snap_count, modes), jnp.float32),
+            pltpu.VMEM((freq_count, 2, 2 * snap_count, modes), jnp.float32),
             pltpu.VMEM((freq_count, ranges, depth_count), jnp.float32),
             pltpu.VMEM((ranges, 1, depth_count), jnp.float32),
             pltpu.VMEM((ranges, 1, depth_count), jnp.float32),

time: 28.3 us -> 25.9 us (0.915)
  Pallas kernels: 26.8 us -> 24.3 us
    pallas_call x1, Pallas kernels: 26.8 us -> 24.3 us  [on_device(): pl.pallas_call(functools.partial(surface_kernel, (groups, tiles, freqs),...]
where the time goes in v1:
time: 25.9 us; the launch traced here: 25.7 us
  Pallas kernels  24.3 us (94%)
  local copies, waits for them, and re-layouts  1.3 us (5%)
    pallas_call x1, Pallas kernels, on_device(): pl.pallas_call(functools.partial(surface_kernel, (groups, tiles, freqs),...  24.3 us
    unnamed x1, local copies, waits for them, and re-layouts  1.3 us

profile of v1, /device:TPU:0, one launch (start us, length us, event | category | flops | bytes accessed | tf_op | source)
XLA Modules:
  0.0 25.7 jit_solution(6487559654470477989)
XLA Ops:
  0.0 24.3 %shard_map.64 = f32[8,1,256]{2,1,0:T(1,128)} custom-call(s32[4]{0:T(128)} %counts.1, s32[3,4,64]{2,1,0:T(4,128)} %bitcast.3, bf16[4,2,256,384]{3,2,1,0:T(8,128)(2,1)} %panels_hbm.1, bf16[4,2,32,256]{3,2,1,0:T(8,128)(2,1)} %snaps_hbm.1, f32[4,384]{1,0:T(4,128)} %wavenumbers_hbm.1, bf16[4,256,384]{2,1,0:T(8,128)(2,1)} %shapes_hbm.1), custom_call_target="tpu_custom_call" | custom-call | tf_op jit(solution)/shard_map/pallas_call | solution.py:304
  24.4 1.3 %copy.8 = f32[1,2048]{1,0:T(1,128)} copy(f32[1,2048]{1,0:T(1,128)} %bitcast.2) | data formatting | bytes 16384
